TPU v7x, 32 devices: a whole 2x2x4 slice. The times are simulated.
32 devices in a mesh: chan: 8 (over y, x, core), seq: 4 (over z).
Axes of the slice: x: 2, y: 2, z: 4, core: 2. Of those that a mesh axis runs over, the one named last changes fastest.
Arguments:
- queries: bfloat16 [8192, 1024], P('chan', 'seq'), may hold values from -6 to 6
- key_rows: bfloat16 [8192, 1024], P('chan', 'seq'), may hold values from -6 to 6
- value_rows: bfloat16 [8192, 1024], P('chan', 'seq'), may hold values from -6 to 6
- filters: float32 [8192, 1024], P('chan', 'seq'), may hold values from -0.1875 to 0.1875
- skip_gain: float32 [8192], P('chan'), may hold values from 0.1 to 1.9
- out_weight: bfloat16 [8192, 4096], P('chan'), may hold values from -0.09375 to 0.09375
Outputs:
- projected: float32 [4096, 1024], P('chan', 'seq')
All inputs are finite; a program needn't handle non-finite values.
Results may differ from a plain program's by a relative error of at most 0.0029.
Values may be sent and summed in bfloat16 or wider, within the bound.
A program may use at most 128 MiB of HBM per device.

v0:
```python
import jax
import jax.numpy as jnp
from jax import lax
from jax.sharding import PartitionSpec as P

highest = lax.Precision.HIGHEST
full_turn = 6.283185307179586


def partner(block, axis, distance):
    count = lax.axis_size(axis)
    route = []
    for low in range(count):
        high = low | 1 << distance
        if high != low and high < count:
            route += [(low, high), (high, low)]
    return lax.ppermute(block, axis, route)


def unit_root(product, count):
    angle = full_turn / count * (product % count).astype(jnp.float32)
    return (jnp.cos(angle), -jnp.sin(angle))


def times_unit(real_part, imag_part, cos_part, sin_part):
    return (
        real_part * cos_part - imag_part * sin_part,
        real_part * sin_part + imag_part * cos_part,
    )


def table_apply(form, table_real, table_imag, data_real, data_imag):
    first = jnp.einsum(form, table_real, data_real, precision=highest) - jnp.einsum(
        form, table_imag, data_imag, precision=highest
    )
    second = jnp.einsum(form, table_real, data_imag, precision=highest) + jnp.einsum(
        form, table_imag, data_real, precision=highest
    )
    return (first, second)


def data_apply(form, data_real, data_imag, table_real, table_imag):
    first = jnp.einsum(form, data_real, table_real, precision=highest) - jnp.einsum(
        form, data_imag, table_imag, precision=highest
    )
    second = jnp.einsum(form, data_imag, table_real, precision=highest) + jnp.einsum(
        form, data_real, table_imag, precision=highest
    )
    return (first, second)


def local_forward(real_part, imag_part):
    length = real_part.shape[-1]
    outer = length // 128
    leading = real_part.shape[:-1]
    grid_real = real_part.reshape(leading + (outer, 128))
    grid_imag = imag_part.reshape(leading + (outer, 128))
    outer_index = jnp.arange(outer, dtype=jnp.int32)
    lane_index = jnp.arange(128, dtype=jnp.int32)
    small_real, small_imag = unit_root(outer_index[:, None] * outer_index[None, :], outer)
    grid_real, grid_imag = table_apply(
        "ka,...ab->...kb", small_real, small_imag, grid_real, grid_imag
    )
    turn_real, turn_imag = unit_root(outer_index[:, None] * lane_index[None, :], length)
    grid_real, grid_imag = times_unit(grid_real, grid_imag, turn_real, turn_imag)
    lane_real, lane_imag = unit_root(lane_index[:, None] * lane_index[None, :], 128)
    grid_real, grid_imag = data_apply("...kb,bc->...kc", grid_real, grid_imag, lane_real, lane_imag)
    return (grid_real.reshape(leading + (length,)), grid_imag.reshape(leading + (length,)))


def local_inverse(real_part, imag_part):
    length = real_part.shape[-1]
    outer = length // 128
    leading = real_part.shape[:-1]
    grid_real = real_part.reshape(leading + (outer, 128))
    grid_imag = imag_part.reshape(leading + (outer, 128))
    outer_index = jnp.arange(outer, dtype=jnp.int32)
    lane_index = jnp.arange(128, dtype=jnp.int32)
    lane_real, lane_imag = unit_root(lane_index[:, None] * lane_index[None, :], 128)
    grid_real, grid_imag = data_apply(
        "...kb,bc->...kc", grid_real, grid_imag, lane_real, -lane_imag
    )
    turn_real, turn_imag = unit_root(outer_index[:, None] * lane_index[None, :], length)
    grid_real, grid_imag = times_unit(grid_real, grid_imag, turn_real, -turn_imag)
    small_real, small_imag = unit_root(outer_index[:, None] * outer_index[None, :], outer)
    grid_real, grid_imag = table_apply(
        "ak,...kb->...ab", small_real, -small_imag, grid_real, grid_imag
    )
    return (grid_real.reshape(leading + (length,)), grid_imag.reshape(leading + (length,)))


def spectral_product(spec_real, spec_imag):
    prod_real = spec_real[0] * spec_real[1] - spec_imag[0] * spec_imag[1]
    prod_imag = spec_real[0] * spec_imag[1] + spec_imag[0] * spec_real[1]
    return (prod_real, prod_imag)


def convolve(signal):
    count = lax.axis_size("seq")
    place = lax.axis_index("seq")
    rows = signal.shape[-1]
    total = 2 * count * rows
    levels = count.bit_length() - 1
    half_cos, half_sin = unit_root(place, 2 * count)
    real_now = jnp.stack([signal, signal * half_cos], axis=2)
    imag_now = jnp.stack([jnp.zeros_like(signal), signal * half_sin], axis=2)
    for level in reversed(range(levels)):
        other_real, other_imag = partner((real_now, imag_now), "seq", level)
        span = 1 << level
        upper = place // span % 2 == 1
        turn_cos, turn_sin = unit_root(place % span, 2 * span)
        rotated_real, rotated_imag = times_unit(
            other_real - real_now, other_imag - imag_now, turn_cos, turn_sin
        )
        real_now = jnp.where(upper, rotated_real, real_now + other_real)
        imag_now = jnp.where(upper, rotated_imag, imag_now + other_imag)
    flipped = jnp.zeros((), jnp.int32)
    for level in range(levels):
        flipped = flipped + place // (1 << level) % 2 * (1 << levels - 1 - level)
    class_base = 2 * flipped
    row_index = jnp.arange(rows, dtype=jnp.int32)
    class_index = class_base + jnp.arange(2, dtype=jnp.int32)
    twist_cos, twist_sin = unit_root(class_index[:, None] * row_index[None, :], total)
    real_now, imag_now = times_unit(real_now, imag_now, twist_cos, twist_sin)
    spec_real, spec_imag = local_forward(real_now, imag_now)
    prod_real, prod_imag = spectral_product(spec_real, spec_imag)
    back_real, back_imag = local_inverse(prod_real, prod_imag)
    back_real, back_imag = times_unit(back_real, back_imag, twist_cos, -twist_sin)
    for level in range(levels):
        other_real, other_imag = partner((back_real, back_imag), "seq", level)
        span = 1 << level
        upper = place // span % 2 == 1
        turn_cos, turn_sin = unit_root(place % span, 2 * span)
        other_rot_real, other_rot_imag = times_unit(other_real, other_imag, turn_cos, -turn_sin)
        self_rot_real, self_rot_imag = times_unit(back_real, back_imag, turn_cos, -turn_sin)
        back_real, back_imag = (
            jnp.where(upper, other_real - self_rot_real, back_real + other_rot_real),
            jnp.where(upper, other_imag - self_rot_imag, back_imag + other_rot_imag),
        )
    result = back_real[:, 0, :] + back_real[:, 1, :] * half_cos + back_imag[:, 1, :] * half_sin
    return result / total


def shards(queries, key_rows, value_rows, filters, skip_gain, out_weight):
    gated = key_rows.astype(jnp.float32) * value_rows.astype(jnp.float32)
    signal = jnp.stack([gated, filters], axis=0)
    conv = convolve(signal)
    mixed = (queries.astype(jnp.float32) * (conv + skip_gain[:, None] * gated)).astype(jnp.bfloat16)
    return lax.psum_scatter(
        lax.dot_general(
            out_weight, mixed, (((0,), (0,)), ((), ())), preferred_element_type=jnp.float32
        ),
        "chan",
        scatter_dimension=0,
        tiled=True,
    )


def solution(mesh):
    placed = (
        P("chan", "seq"),
        P("chan", "seq"),
        P("chan", "seq"),
        P("chan", "seq"),
        P("chan"),
        P("chan", None),
    )
    return jax.shard_map(
        shards, mesh=mesh, in_specs=placed, out_specs=P("chan", "seq"), check_vma=False
    )
```

profile of v0, /device:TPU:0, one launch (start us, length us, event | category | flops | bytes accessed | tf_op | source)
XLA Modules:
  0.0 1082.3 jit_solution(10060734146768786134)
XLA Ops:
  6.7 1.4 fusion.58
  8.7 0.9 copy-done.2
  9.6 2.3 pad_maximum_fusion
  11.9 4.0 collective-permute-start
  16.0 2.3 stack.34
  18.4 269.0 %collective-permute-done = f32[2,1024,2,256]{3,1,2,0:T(8,128)} collective-permute-done((f32[2,1024,2,256]{3,1,2,0:T(8,128)}, f32[2,1024,2,256]{3,1,2,0:T(8,128)}, u32[]{:S(2)}, u32[]{:S(2)}) %collective-permute-start) | collective-permute-done | bytes 4194336 | tf_op jit(solution)/shard_map/ppermute | solution.py:17
  287.4 89.1 %collective-permute-done.1 = f32[2,1024,2,256]{3,1,2,0:T(8,128)} collective-permute-done((f32[2,1024,2,256]{3,1,2,0:T(8,128)}, f32[2,1024,2,256]{3,1,2,0:T(8,128)}, u32[]{:S(2)}, u32[]{:S(2)}) %collective-permute-start.1) | collective-permute-done | bytes 4194336 | tf_op jit(solution)/shard_map/ppermute | solution.py:17
  376.5 7.5 add_select_fusion.2
  384.0 0.7 collective-permute-start.2
  384.7 1.3 collective-permute-start.3
  386.3 91.6 %collective-permute-done.2 = f32[2,1024,2,256]{3,1,2,0:T(8,128)} collective-permute-done((f32[2,1024,2,256]{3,1,2,0:T(8,128)}, f32[2,1024,2,256]{3,1,2,0:T(8,128)}, u32[]{:S(2)}, u32[]{:S(2)}) %collective-permute-start.2) | collective-permute-done | bytes 4194336 | tf_op jit(solution)/shard_map/ppermute | solution.py:17
  477.8 88.1 %collective-permute-done.3 = f32[2,1024,2,256]{3,1,2,0:T(8,128)} collective-permute-done((f32[2,1024,2,256]{3,1,2,0:T(8,128)}, f32[2,1024,2,256]{3,1,2,0:T(8,128)}, u32[]{:S(2)}, u32[]{:S(2)}) %collective-permute-start.3) | collective-permute-done | bytes 4194336 | tf_op jit(solution)/shard_map/ppermute | solution.py:17
  565.9 8.9 multiply_add_fusion
  574.8 2.6 multiply_subtract_fusion
  577.4 5.8 reshape.289
  583.2 5.9 reshape.290
  589.1 16.5 %fusion.11 = f32[2,1024,2,128,2]{3,4,2,1,0:T(2,128)S(1)} fusion(f32[2,1024,2,2,128]{4,3,1,2,0:T(2,128)} %reshape.290), kind=kOutput, calls=%fused_computation.25 | convolution fusion | flops 25165884 | bytes 8388608 | tf_op jit(solution)/shard_map/ka,...ab->...kb/dot_general | solution.py:33
  605.5 15.4 %fusion.13 = f32[2,1024,2,128,2]{3,4,2,1,0:T(2,128)S(1)} fusion(f32[2,1024,2,2,128]{4,3,1,2,0:T(2,128)S(1)} %copy-done.1), kind=kOutput, calls=%fused_computation.27 | convolution fusion | flops 25165884 | bytes 8388608 | tf_op jit(solution)/shard_map/ka,...ab->...kb/dot_general | solution.py:36
  621.0 16.9 %convolution_subtract_fusion = f32[2,1024,2,128,2]{3,4,2,1,0:T(2,128)} fusion(f32[2,1024,2,128,2]{3,4,2,1,0:T(2,128)S(1)} %fusion.11, f32[2,1024,2,2,128]{4,3,1,2,0:T(2,128)S(1)} %copy-done.1), kind=kOutput, calls=%fused_computation.23 | convolution fusion | flops 26214456 | bytes 12582912 | tf_op jit(solution)/shard_map/ka,...ab->...kb/dot_general | solution.py:33
  637.9 20.6 %fusion = (f32[2,1024,2,2,128]{4,3,2,1,0:T(2,128)S(1)}, f32[2,1024,2,2,128]{4,3,2,1,0:T(2,128)S(1)}) fusion(f32[2,1024,2,128,2]{3,4,2,1,0:T(2,128)} %convolution_subtract_fusion, f32[2,128]{1,0:T(2,128)S(1)} %get-tuple-element.28, f32[2,128]{1,0:T(2,128)S(1)} %get-tuple-element.27, f32[2,1024,2,128,2]{3,4,2,1,0:T(2,128)S(1)} %fusion.13, ...), kind=kOutput, calls=%fused_computation.4 | convolution fusion | flops 32505912 | bytes 20973568 | tf_op jit(solution)/shard_map/ka,...ab->...kb/dot_general | solution.py:36
  658.4 3.8 fusion.4
  662.2 3.8 fusion.2
  666.0 3.8 fusion.16
  669.9 4.1 fusion.19
  673.9 0.4 multiply_subtract_fusion.3
  674.4 2.1 fusion.24
  676.5 2.1 fusion.22
  678.6 2.1 fusion.32
  680.8 2.8 multiply_subtract_fusion.2
  683.6 9.8 fusion.42
  693.4 10.7 fusion.38
  704.1 11.6 %subtract_bitcast_fusion = f32[1024,2,2,128]{3,2,1,0:T(2,128)} fusion(f32[1024,2,128,2]{2,3,1,0:T(2,128)S(1)} %fusion.42, f32[1024,2,2,128]{3,0,2,1:T(8,128)S(1)} %get-tuple-element.19), kind=kOutput, calls=%fused_computation.48 | convolution fusion | flops 13107256 | bytes 6291456 | tf_op jit(solution)/shard_map/ak,...kb->...ab/dot_general | solution.py:33
  715.7 4.6 reshape.291
  720.3 12.1 %add_bitcast_fusion = f32[1024,2,2,128]{3,2,1,0:T(2,128)} fusion(f32[1024,2,128,2]{2,3,1,0:T(2,128)} %fusion.38, f32[1024,2,2,128]{3,0,2,1:T(8,128)S(1)} %get-tuple-element.18), kind=kOutput, calls=%fused_computation.47 | convolution fusion | flops 13107256 | bytes 6291456 | tf_op jit(solution)/shard_map/ak,...kb->...ab/dot_general | solution.py:36
  732.4 5.0 reshape.292
  737.5 2.2 multiply_add_fusion.1
  739.6 1.5 collective-permute-start.4
  741.2 0.6 collective-permute-start.5
  741.7 46.5 %collective-permute-done.4 = f32[1024,2,256]{2,0,1:T(8,128)S(1)} collective-permute-done((f32[1024,2,256]{2,0,1:T(8,128)S(1)}, f32[1024,2,256]{2,0,1:T(8,128)S(1)}, u32[]{:S(2)}, u32[]{:S(2)}) %collective-permute-start.4) | collective-permute-done | bytes 2097184 | tf_op jit(solution)/shard_map/ppermute | solution.py:17
  788.3 42.8 %collective-permute-done.5 = f32[1024,2,256]{2,0,1:T(8,128)S(1)} collective-permute-done((f32[1024,2,256]{2,0,1:T(8,128)S(1)}, f32[1024,2,256]{2,0,1:T(8,128)S(1)}, u32[]{:S(2)}, u32[]{:S(2)}) %collective-permute-start.5) | collective-permute-done | bytes 2097184 | tf_op jit(solution)/shard_map/ppermute | solution.py:17
  831.1 0.9 add_select_fusion.5
  832.0 3.8 collective-permute-start.6
  835.9 134.8 %collective-permute-done.6 = f32[1024,2,256]{2,0,1:T(8,128)S(1)} collective-permute-done((f32[1024,2,256]{2,0,1:T(8,128)S(1)}, f32[1024,2,256]{2,0,1:T(8,128)S(1)}, u32[]{:S(2)}, u32[]{:S(2)}) %collective-permute-start.6) | collective-permute-done | bytes 2097184 | tf_op jit(solution)/shard_map/ppermute | solution.py:17
  970.7 44.2 %collective-permute-done.7 = f32[1024,2,256]{2,0,1:T(8,128)S(1)} collective-permute-done((f32[1024,2,256]{2,0,1:T(8,128)S(1)}, f32[1024,2,256]{2,0,1:T(8,128)S(1)}, u32[]{:S(2)}, u32[]{:S(2)}) %collective-permute-start.7) | collective-permute-done | bytes 2097184 | tf_op jit(solution)/shard_map/ppermute | solution.py:17
  1015.0 0.6 add_select_fusion.4
  1015.6 5.2 convolution_bitcast_fusion
  1020.8 52.3 %reduce-scatter.2.cloned.1.call-done = f32[512,256]{0,1:T(8,128)} async-done(((f32[4096,256]{0,1:T(8,128)}), f32[512,256]{0,1:T(8,128)}) %reduce-scatter.2.cloned.1.call-update) | async-done | bytes 524304 | tf_op jit(solution)/shard_map/reduce_scatter | solution.py:149
  1073.1 2.0 copy.23
  (34 shorter events, 0.9 us)
Async XLA Ops:
  6.5 1.6 copy-start.5
  6.5 1066.6 %reduce-scatter.2.cloned.1.call-start = ((), (), s32[]{:S(2)}) async-start(), calls=%async_computation.1 | async-start | bytes 4718592 | tf_op jit(solution)/shard_map/reduce_scatter | solution.py:149
  8.3 1.3 copy-start.2
  8.7 3.2 copy-start.3
  11.9 275.5 %collective-permute-start = (f32[2,1024,2,256]{3,1,2,0:T(8,128)}, f32[2,1024,2,256]{3,1,2,0:T(8,128)}, u32[]{:S(2)}, u32[]{:S(2)}) collective-permute-start(f32[2,1024,2,256]{3,1,2,0:T(8,128)} %pad_maximum_fusion), channel_id=1, source_target_pairs={{0,2},{2,0},{1,3},{3,1},{4,6},{6,4},{5,7},{7,5},{8,10},{10,8},{9,1... | collective-permute-start | bytes 12582920 | tf_op jit(solution)/shard_map/ppermute | solution.py:17
  18.2 358.3 %collective-permute-start.1 = (f32[2,1024,2,256]{3,1,2,0:T(8,128)}, f32[2,1024,2,256]{3,1,2,0:T(8,128)}, u32[]{:S(2)}, u32[]{:S(2)}) collective-permute-start(f32[2,1024,2,256]{3,1,2,0:T(8,128)} %stack.34), channel_id=1, source_target_pairs={{0,2},{2,0},{1,3},{3,1},{4,6},{6,4},{5,7},{7,5},{8,10},{10,8},{9,1... | collective-permute-start | bytes 12582920 | tf_op jit(solution)/shard_map/ppermute | solution.py:17
  384.0 93.8 %collective-permute-start.2 = (f32[2,1024,2,256]{3,1,2,0:T(8,128)}, f32[2,1024,2,256]{3,1,2,0:T(8,128)}, u32[]{:S(2)}, u32[]{:S(2)}) collective-permute-start(f32[2,1024,2,256]{3,1,2,0:T(8,128)} %get-tuple-element.9), channel_id=1, source_target_pairs={{0,1},{1,0},{2,3},{3,2},{4,5},{5,4},{6,7},{7,6},{8,9},{9,8},{10,11... | collective-permute-start | bytes 12582920 | tf_op jit(solution)/shard_map/ppermute | solution.py:17
  384.7 181.2 %collective-permute-start.3 = (f32[2,1024,2,256]{3,1,2,0:T(8,128)}, f32[2,1024,2,256]{3,1,2,0:T(8,128)}, u32[]{:S(2)}, u32[]{:S(2)}) collective-permute-start(f32[2,1024,2,256]{3,1,2,0:T(8,128)} %get-tuple-element.8), channel_id=1, source_target_pairs={{0,1},{1,0},{2,3},{3,2},{4,5},{5,4},{6,7},{7,6},{8,9},{9,8},{10,11... | collective-permute-start | bytes 12582920 | tf_op jit(solution)/shard_map/ppermute | solution.py:17
  589.1 16.5 %copy-start.1 = (f32[2,1024,2,2,128]{4,3,1,2,0:T(2,128)S(1)}, f32[2,1024,2,2,128]{4,3,1,2,0:T(2,128)}, u32[]{:S(2)}) copy-start(f32[2,1024,2,2,128]{4,3,1,2,0:T(2,128)} %reshape.289) | copy-start | bytes 12582916
  621.0 16.9 %copy-start = (f32[2,1024,2,2,128]{4,3,1,2,0:T(2,128)S(1)}, f32[2,1024,2,2,128]{4,3,1,2,0:T(2,128)}, u32[]{:S(2)}) copy-start(f32[2,1024,2,2,128]{4,3,1,2,0:T(2,128)} %reshape.290) | copy-start | bytes 12582916
  732.4 5.0 copy-start.4
  737.4 278.1 %slice-start = ((s8[8388608]{0:T(1024)(128)(4,1)}), s8[4194304]{0:T(1024)(128)(4,1)S(1)}, s32[]{:S(2)}) async-start(s8[8388608]{0:T(1024)(128)(4,1)} %bitcast.122), calls=%async_computation.2 | async-start | bytes 8388608
  739.6 48.6 %collective-permute-start.4 = (f32[1024,2,256]{2,0,1:T(8,128)S(1)}, f32[1024,2,256]{2,0,1:T(8,128)S(1)}, u32[]{:S(2)}, u32[]{:S(2)}) collective-permute-start(f32[1024,2,256]{2,0,1:T(8,128)S(1)} %get-tuple-element.17), channel_id=1, source_target_pairs={{0,1},{1,0},{2,3},{3,2},{4,5},{5,4},{6,7},{7,6},{8,9},{9,8},{10,11... | collective-permute-start | bytes 6291464 | tf_op jit(solution)/shard_map/ppermute | solution.py:17
  741.2 274.4 %slice-start.1 = ((s8[8388608]{0:T(1024)(128)(4,1)}), s8[4194304]{0:T(1024)(128)(4,1)S(1)}, s32[]{:S(2)}) async-start(s8[8388608]{0:T(1024)(128)(4,1)} %bitcast.122), calls=%async_computation.3 | async-start | bytes 8388608
  741.2 89.9 %collective-permute-start.5 = (f32[1024,2,256]{2,0,1:T(8,128)S(1)}, f32[1024,2,256]{2,0,1:T(8,128)S(1)}, u32[]{:S(2)}, u32[]{:S(2)}) collective-permute-start(f32[1024,2,256]{2,0,1:T(8,128)S(1)} %get-tuple-element.16), channel_id=1, source_target_pairs={{0,1},{1,0},{2,3},{3,2},{4,5},{5,4},{6,7},{7,6},{8,9},{9,8},{10,11... | collective-permute-start | bytes 6291464 | tf_op jit(solution)/shard_map/ppermute | solution.py:17
  832.0 138.7 %collective-permute-start.6 = (f32[1024,2,256]{2,0,1:T(8,128)S(1)}, f32[1024,2,256]{2,0,1:T(8,128)S(1)}, u32[]{:S(2)}, u32[]{:S(2)}) collective-permute-start(f32[1024,2,256]{2,0,1:T(8,128)S(1)} %get-tuple-element.13), channel_id=1, source_target_pairs={{0,2},{2,0},{1,3},{3,1},{4,6},{6,4},{5,7},{7,5},{8,10},{10,8},{9,1... | collective-permute-start | bytes 6291464 | tf_op jit(solution)/shard_map/ppermute | solution.py:17
  835.8 179.8 %copy-start.6 = (bf16[1024,256]{1,0:T(8,128)(2,1)S(1)}, bf16[1024,256]{1,0:T(8,128)(2,1)}, u32[]{:S(2)}) copy-start(bf16[1024,256]{1,0:T(8,128)(2,1)} %param.8) | copy-start | bytes 1572868
  835.8 179.8 %copy-start.7 = (bf16[1024,256]{1,0:T(8,128)(2,1)S(1)}, bf16[1024,256]{1,0:T(8,128)(2,1)}, u32[]{:S(2)}) copy-start(bf16[1024,256]{1,0:T(8,128)(2,1)} %param.7) | copy-start | bytes 1572868
  835.8 179.8 %copy-start.8 = (bf16[1024,256]{1,0:T(8,128)(2,1)S(1)}, bf16[1024,256]{1,0:T(8,128)(2,1)}, u32[]{:S(2)}) copy-start(bf16[1024,256]{1,0:T(8,128)(2,1)} %param.6) | copy-start | bytes 1572868
  835.8 179.8 %copy-start.9 = (f32[1024]{0:T(1024)S(1)}, f32[1024]{0:T(1024)}, u32[]{:S(2)}) copy-start(f32[1024]{0:T(1024)} %param.10) | copy-start | bytes 12292
  835.8 179.2 %collective-permute-start.7 = (f32[1024,2,256]{2,0,1:T(8,128)S(1)}, f32[1024,2,256]{2,0,1:T(8,128)S(1)}, u32[]{:S(2)}, u32[]{:S(2)}) collective-permute-start(f32[1024,2,256]{2,0,1:T(8,128)S(1)} %get-tuple-element.12), channel_id=1, source_target_pairs={{0,2},{2,0},{1,3},{3,1},{4,6},{6,4},{5,7},{7,5},{8,10},{10,8},{9,1... | collective-permute-start | bytes 6291464 | tf_op jit(solution)/shard_map/ppermute | solution.py:17
Sparse Core Ops, SparseCore 0:
  1021.0 52.1 reduce-scatter.1
where the time goes:
time: 1100 us; the launch traced here: 1080 us
  waiting for transfers between devices  858 us (78%)
  matrix products  143 us (13%)
  other arithmetic  27.6 us (3%)
  local copies, waits for them, and re-layouts  26.6 us (2%)
  between operations  14.3 us (1%)
  starting transfers between devices  12 us (1%)
    ppermute x8, waiting for transfers between devices, partner(): return lax.ppermute(block, axis, route)  806 us
    reduce_scatter x1, waiting for transfers between devices, shards(): lax.psum_scatter(lax.dot_general(out_weight, mixed, (((0,), (0,)), ((), (...  52.3 us
    dot_general x2, matrix products, table_apply(): jnp.einsum(form, table_real, data_imag, precision=highest)  31.3 us
    dot_general x2, matrix products, table_apply(): jnp.einsum(form, table_imag, data_imag, precision=highest)  28 us
    dot_general x2, matrix products, table_apply(): jnp.einsum(form, table_imag, data_real, precision=highest)  27.5 us
    dot_general x2, matrix products, table_apply(): jnp.einsum(form, table_real, data_real, precision=highest)  26.6 us
  transfers between devices with their start and end apart: 9, of which 9 were waited for; matrix products, arithmetic and copies ran while one was open for 0% of the time, Pallas kernels for 0%

commit v1 on v0

v1 whole, which is shorter than its diff:
```python
import functools

import jax
import jax.numpy as jnp
import ml_dtypes
import numpy as np
from jax import lax
from jax.experimental import pallas as pl
from jax.experimental.pallas import tpu as pltpu
from jax.sharding import PartitionSpec as P

MESH = pl.DeviceIdType.MESH
HALVES = 2
TILE = 256


def tables(length):
    n = np.arange(length, dtype=np.int64)[:, None]
    f = np.arange(length, dtype=np.int64)[None, :]
    angle = np.pi / (2 * length) * (((2 * f + 1) * n) % (4 * length))
    count = length // TILE
    cos = np.cos(angle).reshape(length, count, TILE)
    sin = np.sin(angle).reshape(length, count, TILE)
    both = np.concatenate([cos, sin], axis=2).transpose(1, 0, 2)
    high = both.astype(np.float32).astype(ml_dtypes.bfloat16)
    low = (both - high.astype(np.float64)).astype(np.float32).astype(ml_dtypes.bfloat16)
    return np.stack([high, low], axis=1)


def dot(a, b):
    return lax.dot_general(a, b, (((1,), (0,)), ((), ())), preferred_element_type=jnp.float32)


def dot_t(a, b):
    return lax.dot_general(a, b, (((1,), (1,)), ((), ())), preferred_element_type=jnp.float32)


def kernel(
    zs, chips,
    q_ref, k_ref, v_ref, f_ref, gain_ref, w_hbm, tab_hbm,
    out_ref,
    w_ref, tab_ref, sig_out, sig_in, acc, conv_out, conv_in, mix_hi, mix_lo,
    core_out, core_in, chip_out, chip_in,
    load_sem, sig_send, sig_recv, conv_send, conv_recv, core_send, core_recv, chip_send, chip_recv,
):
    place = lax.axis_index("seq")
    chan = lax.axis_index("chan")
    chip = chan // 2
    core = chan % 2
    other = chip * 2 + (1 - core)
    rows, width = q_ref.shape
    group = rows // zs
    half = group // HALVES
    length = zs * width
    feats = out_ref.shape[1]

    def at(c, s):
        return {"chan": c, "seq": s}

    tab_copy = pltpu.make_async_copy(tab_hbm, tab_ref, load_sem.at[0])
    tab_copy.start()
    w_copy = pltpu.make_async_copy(w_hbm, w_ref, load_sem.at[1])
    w_copy.start()

    barrier = pltpu.get_barrier_semaphore()
    for step in range(1, zs):
        pl.semaphore_signal(barrier, inc=1, device_id=at(chan, (place + step) % zs), device_id_type=MESH)
    for step in range(1, chips):
        pl.semaphore_signal(
            barrier, inc=1, device_id=at((chip + step) % chips * 2 + core, place), device_id_type=MESH
        )
    pl.semaphore_signal(barrier, inc=1, device_id=at(other, place), device_id_type=MESH)

    for j in range(zs):
        for h in range(HALVES):
            here = pl.ds(j * group + h * half, half)
            g = k_ref[here, :].astype(jnp.float32) * v_ref[here, :].astype(jnp.float32)
            sig_out[h, j, 0] = g.astype(jnp.bfloat16)
            sig_out[h, j, 1] = f_ref[here, :].astype(jnp.bfloat16)

    pl.semaphore_wait(barrier, zs + chips - 1)

    columns = pl.ds(pl.multiple_of(place * width, width), width)
    sends = []
    for h in range(HALVES):
        for step in range(1, zs):
            to = (place + step) % zs
            copy = pltpu.make_async_remote_copy(
                src_ref=sig_out.at[h, to],
                dst_ref=sig_in.at[h, :, :, columns],
                send_sem=sig_send.at[h, step],
                recv_sem=sig_recv.at[h, step],
                device_id=at(chan, to),
                device_id_type=MESH,
            )
            copy.start()
            sends.append(copy)
    for h in range(HALVES):
        sig_in[h, :, :, columns] = sig_out[h, place]

    tab_copy.wait()
    backs = []
    for h in range(HALVES):
        for step in range(1, zs):
            sends[h * (zs - 1) + step - 1].wait_recv()
        acc[...] = jnp.zeros_like(acc)

        def tile(i, carry):
            both = sig_in[h].reshape(2 * half, length)
            spec = dot(both, tab_ref[i, 0]) + dot(both, tab_ref[i, 1])
            ga, gb = spec[:half, :TILE], spec[:half, TILE:]
            fa, fb = spec[half:, :TILE], spec[half:, TILE:]
            prod = jnp.concatenate([ga * fa - gb * fb, ga * fb + gb * fa], axis=1)
            high = prod.astype(jnp.bfloat16)
            low = (prod - high.astype(jnp.float32)).astype(jnp.bfloat16)
            acc[...] += (
                dot_t(high, tab_ref[i, 0]) + dot_t(low, tab_ref[i, 0]) + dot_t(high, tab_ref[i, 1])
            )
            return carry

        lax.fori_loop(0, length // TILE, tile, 0)
        for j in range(zs):
            conv_out[h, j] = (acc[:, j * width : (j + 1) * width] * (1.0 / length)).astype(jnp.bfloat16)
        for step in range(1, zs):
            to = (place + step) % zs
            copy = pltpu.make_async_remote_copy(
                src_ref=conv_out.at[h, to],
                dst_ref=conv_in.at[place, h],
                send_sem=conv_send.at[h, step],
                recv_sem=conv_recv.at[h, step],
                device_id=at(chan, to),
                device_id_type=MESH,
            )
            copy.start()
            backs.append(copy)
        conv_in[place, h] = conv_out[h, place]

    for copy in backs:
        copy.wait_recv()
    for j in range(zs):
        for h in range(HALVES):
            start = j * group + h * half
            here = pl.ds(start, half)
            g = k_ref[here, :].astype(jnp.float32) * v_ref[here, :].astype(jnp.float32)
            total = conv_in[j, h].astype(jnp.float32) + gain_ref[here, :] * g
            mixed = (q_ref[here, :].astype(jnp.float32) * total).T
            high = mixed.astype(jnp.bfloat16)
            mix_hi[:, here] = high
            mix_lo[:, here] = (mixed - high.astype(jnp.float32)).astype(jnp.bfloat16)

    w_copy.wait()

    def part(target):
        w = w_ref[:, pl.ds(pl.multiple_of(target * feats, feats), feats)]
        return dot(mix_hi[...], w) + dot(mix_lo[...], w)

    cores = []
    for step in range(chips):
        d = (chip + 1 + step) % chips
        core_out[step] = part(d * 2 + (1 - core))
        copy = pltpu.make_async_remote_copy(
            src_ref=core_out.at[step],
            dst_ref=core_in.at[step],
            send_sem=core_send.at[step],
            recv_sem=core_recv.at[step],
            device_id=at(other, place),
            device_id_type=MESH,
        )
        copy.start()
        cores.append(copy)
    hops = []
    for step in range(chips):
        d = (chip + 1 + step) % chips
        mine = part(d * 2 + core)
        cores[step].wait_recv()
        mine = mine + core_in[step]
        if step < chips - 1:
            chip_out[step] = mine.astype(jnp.bfloat16)
            copy = pltpu.make_async_remote_copy(
                src_ref=chip_out.at[step],
                dst_ref=chip_in.at[step],
                send_sem=chip_send.at[step],
                recv_sem=chip_recv.at[step],
                device_id=at(d * 2 + core, place),
                device_id_type=MESH,
            )
            copy.start()
            hops.append(copy)
        else:
            out_ref[...] = mine
    for step in range(chips - 1):
        hops[step].wait_recv()
        out_ref[...] += chip_in[step].astype(jnp.float32)
    for copy in sends + backs + cores + hops:
        copy.wait_send()


def shards(zs, chans, queries, key_rows, value_rows, filters, skip_gain, out_weight):
    rows, width = queries.shape
    chips = chans // 2
    length = zs * width
    group = rows // zs
    half = group // HALVES
    features = out_weight.shape[1]
    feats = features // chans
    table = jnp.asarray(tables(length))
    vmem = pl.BlockSpec(memory_space=pltpu.VMEM)
    hbm = pl.BlockSpec(memory_space=pl.ANY)
    dma = pltpu.SemaphoreType.DMA
    bf16, f32 = jnp.bfloat16, jnp.float32
    out = pl.pallas_call(
        functools.partial(kernel, zs, chips),
        out_shape=jax.ShapeDtypeStruct((width, feats), f32),
        in_specs=[vmem] * 5 + [hbm] * 2,
        out_specs=vmem,
        scratch_shapes=[
            pltpu.VMEM((rows, features), bf16),
            pltpu.VMEM(table.shape, bf16),
            pltpu.VMEM((HALVES, zs, 2, half, width), bf16),
            pltpu.VMEM((HALVES, 2, half, length), bf16),
            pltpu.VMEM((half, length), f32),
            pltpu.VMEM((HALVES, zs, half, width), bf16),
            pltpu.VMEM((zs, HALVES, half, width), bf16),
            pltpu.VMEM((width, rows), bf16),
            pltpu.VMEM((width, rows), bf16),
            pltpu.VMEM((chips, width, feats), f32),
            pltpu.VMEM((chips, width, feats), f32),
            pltpu.VMEM((chips, width, feats), bf16),
            pltpu.VMEM((chips, width, feats), bf16),
            dma((2,)),
            dma((HALVES, zs)),
            dma((HALVES, zs)),
            dma((HALVES, zs)),
            dma((HALVES, zs)),
            dma((chips,)),
            dma((chips,)),
            dma((chips,)),
            dma((chips,)),
        ],
        compiler_params=pltpu.CompilerParams(
            collective_id=0, has_side_effects=True, vmem_limit_bytes=56 * 2**20
        ),
    )(queries, key_rows, value_rows, filters, skip_gain[:, None], out_weight, table)
    return out.T


def solution(mesh):
    placed = (
        P("chan", "seq"),
        P("chan", "seq"),
        P("chan", "seq"),
        P("chan", "seq"),
        P("chan"),
        P("chan", None),
    )
    return jax.shard_map(
        functools.partial(shards, mesh.shape["seq"], mesh.shape["chan"]),
        mesh=mesh,
        in_specs=placed,
        out_specs=P("chan", "seq"),
        check_vma=False,
    )
```

time: 1100 us -> 68.2 us (0.06); the launches traced: 1080 us -> 68 us
  waiting for transfers between devices: 858 us -> 0 us
  matrix products: 143 us -> 0 us
  Pallas kernels: 0 us -> 64.2 us
  other arithmetic: 27.6 us -> 0 us
  local copies, waits for them, and re-layouts: 26.6 us -> 3.74 us
  between operations: 14.3 us -> 0.01 us
  starting transfers between devices: 12 us -> 0 us
    ppermute x8 -> x0, waiting for transfers between devices: 806 us -> none  [partner(): return lax.ppermute(block, axis, route)]
    dot_general x17 -> x0, matrix products: 143 us -> none  [the longest x2 31.3 us: table_apply(): jnp.einsum(form, table_real, data_imag, precision=highest)]
    pallas_call x0 -> x1, Pallas kernels: none -> 64.2 us  [shards(): pl.pallas_call(functools.partial(kernel, zs, chips), out_shape=jax.ShapeD...]
    reduce_scatter x1 -> x0, waiting for transfers between devices: 52.3 us -> none  [shards(): lax.psum_scatter(lax.dot_general(out_weight, mixed, (((0,), (0,)), ((), (...]
    reshape x4 -> x0, local copies, waits for them, and re-layouts: 21.3 us -> none  [the longest x1 5.86 us: local_forward(): grid_imag = imag_part.reshape(leading + (outer, 128))]
    ppermute x8 -> x0, starting transfers between devices: 12 us -> none  [partner(): return lax.ppermute(block, axis, route)]
    add x3 -> x0, other arithmetic: 11.1 us -> none  [the longest x2 11.1 us: times_unit(): real_part * sin_part + imag_part * cos_part]
  transfers between devices with their start and end apart: 9 -> 0, of which waited for: 9 -> 0; matrix products, arithmetic and copies ran while one was open for 0% -> 0% of each run, Pallas kernels for 0% -> 0%
where the time goes in v1:
time: 68.2 us; the launch traced here: 68 us
  Pallas kernels  64.2 us (94%)
  local copies, waits for them, and re-layouts  3.74 us (5%)
    pallas_call x1, Pallas kernels, shards(): pl.pallas_call(functools.partial(kernel, zs, chips), out_shape=jax.ShapeD...  64.2 us
    transpose x1, local copies, waits for them, and re-layouts, shards(): return out.T  2.04 us
    broadcast_in_dim x1, local copies, waits for them, and re-layouts, shards(): skip_gain[:, None]  1.71 us

profile of v1, /device:TPU:0, one launch (start us, length us, event | category | flops | bytes accessed | tf_op | source)
XLA Modules:
  0.0 68.0 jit_solution(1725616310437631406)
XLA Ops:
  0.0 1.7 %copy.9.gain_ref = f32[1024,1]{1,0:T(8,128)} copy(f32[1024,1]{0,1:T(1,128)} %bitcast.3) | data formatting | bytes 8192 | tf_op jit(solution)/shard_map/broadcast_in_dim | solution.py:243
  1.7 64.2 %shard_map.73 = f32[256,512]{1,0:T(8,128)} custom-call(bf16[1024,256]{1,0:T(8,128)(2,1)} %q_ref.1, bf16[1024,256]{1,0:T(8,128)(2,1)} %k_ref.1, bf16[1024,256]{1,0:T(8,128)(2,1)} %v_ref.1, f32[1024,256]{1,0:T(8,128)} %f_ref.1, f32[1024,1]{1,0:T(8,128)} %copy.9.gain_ref, bf16[1024,4096]{1,0:T(8,128)(2,1)} %w_hbm.1, bf16[4,2,1024,512]{3,2,1,0:T(8,128)(2,1)} %constant.2.clone.tab_hbm), custom_call_target="tpu_custom_call" | custom-call | tf_op jit(solution)/shard_map/pallas_call | solution.py:211
  65.9 2.0 %copy.10 = f32[512,256]{1,0:T(8,128)} copy(f32[512,256]{0,1:T(8,128)} %bitcast.2) | data formatting | bytes 1048576 | tf_op jit(solution)/shard_map/transpose | solution.py:244

commit v2 on v1

v2 whole, which is shorter than its diff:
```python
import functools

import jax
import jax.numpy as jnp
import ml_dtypes
import numpy as np
from jax import lax
from jax.experimental import pallas as pl
from jax.experimental.pallas import tpu as pltpu
from jax.sharding import PartitionSpec as P

MESH = pl.DeviceIdType.MESH
HALVES = 2
TILE = 256


def tables(length):
    n = np.arange(length, dtype=np.int64)[:, None]
    f = np.arange(length, dtype=np.int64)[None, :]
    angle = np.pi / (2 * length) * (((2 * f + 1) * n) % (4 * length))
    count = length // TILE
    cos = np.cos(angle).reshape(length, count, TILE)
    sin = np.sin(angle).reshape(length, count, TILE)
    both = np.concatenate([cos, sin], axis=2).transpose(1, 0, 2)
    high = both.astype(np.float32).astype(ml_dtypes.bfloat16)
    low = (both - high.astype(np.float64)).astype(np.float32).astype(ml_dtypes.bfloat16)
    return np.stack([high, low], axis=1)


def dot(a, b):
    return lax.dot_general(a, b, (((1,), (0,)), ((), ())), preferred_element_type=jnp.float32)


def dot_t(a, b):
    return lax.dot_general(a, b, (((1,), (1,)), ((), ())), preferred_element_type=jnp.float32)


def kernel(
    zs, chips, halves,
    q_ref, k_ref, v_ref, f_ref, gain_ref, w_hbm, tab_hbm,
    out_ref,
    w_ref, tab_ref, sig_out, sig_in, acc, conv_out, conv_in, skip, mix_hi, mix_lo, own,
    core_out, core_in, chip_out, chip_in,
    tab_sem, w_sem, sig_send, sig_recv, conv_send, conv_recv,
    core_send, core_recv, chip_send, chip_recv,
):
    place = lax.axis_index("seq")
    chan = lax.axis_index("chan")
    chip = chan // 2
    core = chan % 2
    other = chip * 2 + (1 - core)
    rows, width = q_ref.shape
    group = rows // zs
    half = group // halves
    length = zs * width
    feats = out_ref.shape[0]
    pieces, piece = conv_out.shape[2], conv_out.shape[4]

    def at(c, s):
        return {"chan": c, "seq": s}

    barrier = pltpu.get_barrier_semaphore()
    for step in range(1, zs):
        pl.semaphore_signal(barrier, inc=1, device_id=at(chan, (place + step) % zs), device_id_type=MESH)
    for step in range(1, chips):
        pl.semaphore_signal(
            barrier, inc=1, device_id=at((chip + step) % chips * 2 + core, place), device_id_type=MESH
        )
    pl.semaphore_signal(barrier, inc=1, device_id=at(other, place), device_id_type=MESH)

    tab_copy = pltpu.make_async_copy(tab_hbm, tab_ref, tab_sem)
    tab_copy.start()
    w_copies = []
    for h in range(halves):
        for j in range(zs):
            copy = pltpu.make_async_copy(
                w_hbm.at[pl.ds(j * group + h * half, half), :],
                w_ref.at[h, pl.ds(j * half, half), :],
                w_sem.at[h, j],
            )
            copy.start()
            w_copies.append(copy)

    columns = pl.ds(pl.multiple_of(place * width, width), width)
    sends = []
    for h in range(halves):
        for j in range(zs):
            here = pl.ds(j * group + h * half, half)
            g = k_ref[here, :].astype(jnp.float32) * v_ref[here, :].astype(jnp.float32)
            sig_out[h, j, 0] = g.astype(jnp.bfloat16)
            sig_out[h, j, 1] = f_ref[here, :].astype(jnp.bfloat16)
        if h == 0:
            pl.semaphore_wait(barrier, zs + chips - 1)
        for step in range(1, zs):
            to = (place + step) % zs
            copy = pltpu.make_async_remote_copy(
                src_ref=sig_out.at[h, to],
                dst_ref=sig_in.at[h, :, :, columns],
                send_sem=sig_send.at[h, step],
                recv_sem=sig_recv.at[h, step],
                device_id=at(chan, to),
                device_id_type=MESH,
            )
            copy.start()
            sends.append(copy)
    for h in range(halves):
        sig_in[h, :, :, columns] = sig_out[h, place]

    for r in range(rows // 128):
        here = pl.ds(r * 128, 128)
        gain = jnp.broadcast_to(gain_ref[r : r + 1, :], (128, 128)).T[:, :1]
        skip[here, :] = gain * (k_ref[here, :].astype(jnp.float32) * v_ref[here, :].astype(jnp.float32))

    def part(h, target, span):
        w = w_ref[h, :, pl.ds(pl.multiple_of(target * feats, feats), feats)]
        return dot(mix_hi[h, span], w) + dot(mix_lo[h, span], w)

    def span_of(p):
        return pl.ds(p * piece, piece)

    def chip_at(step):
        return (chip + 1 + step) % chips

    def mix(h, p):
        span = span_of(p)
        for step in range(1, zs):
            backs[(h * pieces + p) * (zs - 1) + step - 1].wait_recv()
        for j in range(zs):
            here = pl.ds(j * group + h * half, half)
            total = conv_in[j, h, p].astype(jnp.float32) + skip[here, span]
            mixed = (q_ref[here, span].astype(jnp.float32) * total).T
            high = mixed.astype(jnp.bfloat16)
            mix_hi[h, span, j * half : (j + 1) * half] = high
            mix_lo[h, span, j * half : (j + 1) * half] = (mixed - high.astype(jnp.float32)).astype(jnp.bfloat16)

    def early(h):
        for p in range(pieces):
            mix(h, p)
        for step in range(chips):
            first = part(h, chip_at(step) * 2 + (1 - core), slice(None))
            second = part(h, chip_at(step) * 2 + core, slice(None))
            core_out[step] = first if h == 0 else core_out[step] + first
            own[step] = second if h == 0 else own[step] + second

    tab_copy.wait()
    for copy in w_copies:
        copy.wait()
    backs = []
    for h in range(halves):
        for step in range(1, zs):
            sends[h * (zs - 1) + step - 1].wait_recv()
        acc[...] = jnp.zeros_like(acc)

        def tile(i, carry):
            both = sig_in[h].reshape(2 * half, length)
            spec = dot(both, tab_ref[i, 0]) + dot(both, tab_ref[i, 1])
            ga, gb = spec[:half, :TILE], spec[:half, TILE:]
            fa, fb = spec[half:, :TILE], spec[half:, TILE:]
            prod = jnp.concatenate([ga * fa - gb * fb, ga * fb + gb * fa], axis=1)
            high = prod.astype(jnp.bfloat16)
            low = (prod - high.astype(jnp.float32)).astype(jnp.bfloat16)
            acc[...] += (
                dot_t(high, tab_ref[i, 0]) + dot_t(low, tab_ref[i, 0]) + dot_t(high, tab_ref[i, 1])
            )
            return carry

        lax.fori_loop(0, length // TILE, tile, 0)
        for j in range(zs):
            for p in range(pieces):
                start = j * width + p * piece
                conv_out[h, j, p] = (acc[:, start : start + piece] * (1.0 / length)).astype(jnp.bfloat16)
        for p in range(pieces):
            for step in range(1, zs):
                to = (place + step) % zs
                copy = pltpu.make_async_remote_copy(
                    src_ref=conv_out.at[h, to, p],
                    dst_ref=conv_in.at[place, h, p],
                    send_sem=conv_send.at[h, p, step],
                    recv_sem=conv_recv.at[h, p, step],
                    device_id=at(chan, to),
                    device_id_type=MESH,
                )
                copy.start()
                backs.append(copy)
        conv_in[place, h] = conv_out[h, place]
        if h == halves - 1:
            for early_h in range(halves - 1):
                early(early_h)

    last = halves - 1
    cores, hops = [], []

    def to_core(p, step):
        span = span_of(p)
        core_out[step, span] += part(last, chip_at(step) * 2 + (1 - core), span)
        copy = pltpu.make_async_remote_copy(
            src_ref=core_out.at[step, span],
            dst_ref=core_in.at[step, span],
            send_sem=core_send.at[p, step],
            recv_sem=core_recv.at[p, step],
            device_id=at(other, place),
            device_id_type=MESH,
        )
        copy.start()
        cores.append(copy)

    def to_chip(p, step):
        span = span_of(p)
        mine = own[step, span] + part(last, chip_at(step) * 2 + core, span)
        cores[p * chips + step].wait_recv()
        mine = (mine + core_in[step, span]).T
        if step == chips - 1:
            out_ref[:, span] = mine
            return
        chip_out[p, step] = mine.astype(jnp.bfloat16)
        copy = pltpu.make_async_remote_copy(
            src_ref=chip_out.at[p, step],
            dst_ref=chip_in.at[p, step],
            send_sem=chip_send.at[p, step],
            recv_sem=chip_recv.at[p, step],
            device_id=at(chip_at(step) * 2 + core, place),
            device_id_type=MESH,
        )
        copy.start()
        hops.append(copy)

    for p in range(pieces):
        mix(last, p)
        to_core(p, 0)
        for step in range(1, chips):
            to_core(p, step)
            to_chip(p, step - 1)
        to_chip(p, chips - 1)
    for p in range(pieces):
        for step in range(chips - 1):
            hops[p * (chips - 1) + step].wait_recv()
            out_ref[:, span_of(p)] += chip_in[p, step].astype(jnp.float32)
    for copy in sends + backs + cores + hops:
        copy.wait_send()


def shards(zs, chans, queries, key_rows, value_rows, filters, skip_gain, out_weight):
    rows, width = queries.shape
    chips = chans // 2
    length = zs * width
    group = rows // zs
    halves = HALVES if group % (16 * HALVES) == 0 else 1
    half = group // halves
    pieces = 2 if width % 256 == 0 else 1
    piece = width // pieces
    features = out_weight.shape[1]
    feats = features // chans
    table = jnp.asarray(tables(length))
    vmem = pl.BlockSpec(memory_space=pltpu.VMEM)
    hbm = pl.BlockSpec(memory_space=pl.ANY)
    dma = pltpu.SemaphoreType.DMA
    bf16, f32 = jnp.bfloat16, jnp.float32
    out = pl.pallas_call(
        functools.partial(kernel, zs, chips, halves),
        out_shape=jax.ShapeDtypeStruct((feats, width), f32),
        in_specs=[vmem] * 5 + [hbm] * 2,
        out_specs=vmem,
        scratch_shapes=[
            pltpu.VMEM((halves, zs * half, features), bf16),
            pltpu.VMEM(table.shape, bf16),
            pltpu.VMEM((halves, zs, 2, half, width), bf16),
            pltpu.VMEM((halves, 2, half, length), bf16),
            pltpu.VMEM((half, length), f32),
            pltpu.VMEM((halves, zs, pieces, half, piece), bf16),
            pltpu.VMEM((zs, halves, pieces, half, piece), bf16),
            pltpu.VMEM((rows, width), f32),
            pltpu.VMEM((halves, width, zs * half), bf16),
            pltpu.VMEM((halves, width, zs * half), bf16),
            pltpu.VMEM((chips, width, feats), f32),
            pltpu.VMEM((chips, width, feats), f32),
            pltpu.VMEM((chips, width, feats), f32),
            pltpu.VMEM((pieces, chips, feats, piece), bf16),
            pltpu.VMEM((pieces, chips, feats, piece), bf16),
            dma,
            dma((halves, zs)),
            dma((halves, zs)),
            dma((halves, zs)),
            dma((halves, pieces, zs)),
            dma((halves, pieces, zs)),
            dma((pieces, chips)),
            dma((pieces, chips)),
            dma((pieces, chips)),
            dma((pieces, chips)),
        ],
        compiler_params=pltpu.CompilerParams(
            collective_id=0, has_side_effects=True, vmem_limit_bytes=56 * 2**20
        ),
    )(queries, key_rows, value_rows, filters, skip_gain.reshape(-1, 128), out_weight, table)
    return out


def solution(mesh):
    placed = (
        P("chan", "seq"),
        P("chan", "seq"),
        P("chan", "seq"),
        P("chan", "seq"),
        P("chan"),
        P("chan", None),
    )
    return jax.shard_map(
        functools.partial(shards, mesh.shape["seq"], mesh.shape["chan"]),
        mesh=mesh,
        in_specs=placed,
        out_specs=P("chan", "seq"),
        check_vma=False,
    )
```

time: 68.2 us -> 64.4 us (0.944)
  local copies, waits for them, and re-layouts: 3.74 us -> 1.87 us
  Pallas kernels: 64.2 us -> 62.4 us
    transpose x1 -> x0, local copies, waits for them, and re-layouts: 2.04 us -> none  [shards(): return out.T]
    unnamed x0 -> x1, local copies, waits for them, and re-layouts: none -> 1.87 us
    pallas_call x1, Pallas kernels: 64.2 us -> 62.4 us  [shards(): pl.pallas_call(functools.partial(kernel, zs, chips, halves), out_shape=ja...]
    broadcast_in_dim x1 -> x0, local copies, waits for them, and re-layouts: 1.71 us -> none  [shards(): skip_gain[:, None]]
where the time goes in v2:
time: 64.4 us; the launch traced here: 64.2 us
  Pallas kernels  62.4 us (97%)
  local copies, waits for them, and re-layouts  1.87 us (3%)
    pallas_call x1, Pallas kernels, shards(): pl.pallas_call(functools.partial(kernel, zs, chips, halves), out_shape=ja...  62.4 us
    unnamed x1, local copies, waits for them, and re-layouts  1.87 us

profile of v2, /device:TPU:0, one launch (start us, length us, event | category | flops | bytes accessed | tf_op | source)
XLA Modules:
  0.0 64.2 jit_solution(14418610143135335045)
XLA Ops:
  0.0 62.4 %shard_map.73 = f32[512,256]{1,0:T(8,128)} custom-call(bf16[1024,256]{1,0:T(8,128)(2,1)} %q_ref.1, bf16[1024,256]{1,0:T(8,128)(2,1)} %k_ref.1, bf16[1024,256]{1,0:T(8,128)(2,1)} %v_ref.1, f32[1024,256]{1,0:T(8,128)} %f_ref.1, f32[8,128]{1,0:T(8,128)} %bitcast.1, bf16[1024,4096]{1,0:T(8,128)(2,1)} %w_hbm.1, bf16[4,2,1024,512]{3,2,1,0:T(8,128)(2,1)} %constant.2.clone.tab_hbm), custom_call_target="tpu_custom_call" | custom-call | tf_op jit(solution)/shard_map/pallas_call | solution.py:258
  62.4 1.9 %copy.9 = f32[512,256]{1,0:T(8,128)} copy(f32[512,256]{1,0:T(8,128)} %shard_map.73) | data formatting | bytes 1048576
